TPU v7x, 128 devices: a whole 4x4x4 slice. The times are simulated.
128 devices in a mesh: expert: 16 (over z_lo, x, core), etp: 8 (over y, z_hi).
Axes of the slice: x: 4, y: 4, z: 4 (z_hi: 2, z_lo: 2; z = z_hi * 2 + z_lo), core: 2. Of those that a mesh axis runs over, the one named last changes fastest.
Arguments:
- tokens: bfloat16 [16384, 4096], P(('expert', 'etp')), may hold values from -6 to 6
- grad_out: bfloat16 [16384, 4096], P(('expert', 'etp')), may hold values from -6 to 6
- route_prob: float32 [16384], P(('expert', 'etp')), may hold values from 0.1 to 1
- expert_index: int32 [16384, 1], P(('expert', 'etp')), may hold values from 0 to 15; in each aligned block of 128 rows (0 to 127, 128 to 255, ...) at most 16 rows name the same one
- w_gate: bfloat16 [16, 4096, 4096], P('expert', None, 'etp'), may hold values from -0.09375 to 0.09375
- w_up: bfloat16 [16, 4096, 4096], P('expert', None, 'etp'), may hold values from -0.09375 to 0.09375
- w_down: bfloat16 [16, 4096, 4096], P('expert', 'etp'), may hold values from -0.09375 to 0.09375
Outputs:
- grad_tokens: bfloat16 [16384, 4096], P(('expert', 'etp'))
Inputs may be any that keep to these rules, and one draw needn't show every extreme that they name: `expert_index`: in the 128 rows of one device no expert is named more than 16 times, a bound that some block reaches.
All inputs are finite; a program needn't handle non-finite values.
Results may differ from a plain program's by a relative error of at most 0.015.
Values may be sent and summed in bfloat16 or wider, within the bound.
A program may use at most 192 MiB of HBM per device.

v0:
```python
import jax
import jax.numpy as jnp
from jax import lax
from jax.sharding import PartitionSpec as P


def expert_terms(rows_x, rows_grad, gate_local, up_local, down_local):
    gate_proj = jnp.dot(rows_x, gate_local, preferred_element_type=jnp.float32)
    up_proj = jnp.dot(rows_x, up_local, preferred_element_type=jnp.float32)
    hidden_grad = jnp.dot(rows_grad, down_local.T, preferred_element_type=jnp.float32)
    sigma = jax.nn.sigmoid(gate_proj)
    slope = sigma * (1.0 + gate_proj * (1.0 - sigma))
    gate_grad = (hidden_grad * up_proj * slope).astype(jnp.bfloat16)
    up_grad = (hidden_grad * gate_proj * sigma).astype(jnp.bfloat16)
    return jnp.dot(gate_grad, gate_local.T, preferred_element_type=jnp.float32) + jnp.dot(
        up_grad, up_local.T, preferred_element_type=jnp.float32
    )


def shards(tokens, grad_out, route_prob, expert_index, w_gate, w_up, w_down):
    experts = lax.axis_size("expert")
    members = lax.axis_size("etp")
    tok_rows, features = tokens.shape
    groups = experts * members
    capacity = members * ((tok_rows * 5 // 4 + groups - 1) // groups)
    expert_ids = expert_index[:, 0]
    chosen = (expert_ids[:, None] == jnp.arange(experts, dtype=jnp.int32)[None, :]).astype(
        jnp.int32
    )
    before = jnp.cumsum(chosen, axis=0) - chosen
    slot_place = expert_ids * capacity + jnp.sum(before * chosen, axis=1)
    scaled = (route_prob[:, None] * grad_out.astype(jnp.float32)).astype(jnp.bfloat16)
    send_rows = jnp.zeros((experts * capacity, features), jnp.bfloat16).at[slot_place].set(tokens)
    send_grads = jnp.zeros((experts * capacity, features), jnp.bfloat16).at[slot_place].set(scaled)
    own_rows, own_grads = (
        lax.all_to_all(
            send_rows.reshape(experts, capacity, features),
            "expert",
            split_axis=0,
            concat_axis=0,
            tiled=True,
        ),
        lax.all_to_all(
            send_grads.reshape(experts, capacity, features),
            "expert",
            split_axis=0,
            concat_axis=0,
            tiled=True,
        ),
    )
    group_x, group_grad = (
        lax.all_gather(own_rows.reshape(-1, features), "etp", axis=0, tiled=True),
        lax.all_gather(own_grads.reshape(-1, features), "etp", axis=0, tiled=True),
    )
    gate_local = w_gate[0]
    up_local = w_up[0]
    down_local = w_down[0]
    summed = lax.psum_scatter(
        expert_terms(group_x, group_grad, gate_local, up_local, down_local).astype(jnp.bfloat16),
        "etp",
        scatter_dimension=0,
        tiled=True,
    )
    returned = lax.all_to_all(
        summed.reshape(experts, capacity, features),
        "expert",
        split_axis=0,
        concat_axis=0,
        tiled=True,
    )
    return returned.reshape(-1, features)[slot_place]


def solution(mesh):
    return jax.shard_map(
        shards,
        mesh=mesh,
        in_specs=(
            P(("expert", "etp"), None),
            P(("expert", "etp"), None),
            P(("expert", "etp")),
            P(("expert", "etp"), None),
            P("expert", None, "etp"),
            P("expert", None, "etp"),
            P("expert", "etp", None),
        ),
        out_specs=P(("expert", "etp"), None),
        check_vma=False,
    )
```

profile of v0, /device:TPU:96, one launch (start us, length us, event | category | flops | bytes accessed | tf_op | source)
XLA Modules:
  0.0 737.4 jit_solution(1589957046741932969)
XLA Ops:
  6.5 0.0 all-gather.5.cloned.1.call-start
  6.5 0.7 fusion.20
  7.3 0.2 reduce_window_sum.11
  7.5 0.8 select_reduce_fusion
  8.3 0.7 fusion.21
  9.0 0.0 copy-start
  9.0 0.0 copy-start.1
  9.0 3.5 scatter_custom_fusion.1
  12.4 32.0 %all_to_all.15 = bf16[16,16,4096]{2,1,0:T(8,128)(2,1)} all-to-all(bf16[16,16,4096]{2,1,0:T(8,128)(2,1)S(1)} %bitcast.37), channel_id=1, replica_groups=mesh['expert'=16,'etp'=8] {'expert'}, dimensions={0} | all-to-all | bytes 4194304 | tf_op jit(solution)/shard_map/all_to_all | solution.py:36
  44.5 0.0 all-gather.5.cloned.1.call-update
  44.5 0.0 all-gather.3.cloned.1.call-start
  44.5 0.0 copy-done
  44.5 0.0 copy-done.1
  44.5 2.8 scatter_custom_fusion
  47.3 31.3 %all_to_all.16 = bf16[16,16,4096]{2,1,0:T(8,128)(2,1)} all-to-all(bf16[16,16,4096]{2,1,0:T(8,128)(2,1)S(1)} %bitcast.36), channel_id=1, replica_groups=mesh['expert'=16,'etp'=8] {'expert'}, dimensions={0} | all-to-all | bytes 4194304 | tf_op jit(solution)/shard_map/all_to_all | solution.py:43
  78.7 0.0 all-gather.3.cloned.1.call-update
  78.7 0.2 reduce-scatter.2.cloned.1.call-start
  78.9 167.6 %all-gather.5.cloned.1.call-done = bf16[2048,4096]{1,0:T(8,128)(2,1)} async-done(((bf16[256,4096]{1,0:T(8,128)(2,1)}), bf16[2048,4096]{1,0:T(8,128)(2,1)}) %all-gather.5.cloned.1.call-update) | async-done | bytes 16777232 | tf_op jit(solution)/shard_map/all_gather | solution.py:52
  246.6 14.9 %fusion.2 = f32[2048,512]{1,0:T(8,128)} fusion(bf16[2048,4096]{1,0:T(8,128)(2,1)} %all-gather.5.cloned.1.call-done, bf16[1,4096,512]{2,1,0:T(8,128)(2,1)} %param.11), kind=kOutput, calls=%fused_computation.6 | convolution fusion | flops 8589934592 | bytes 25165824 | tf_op jit(solution)/shard_map/dot_general | solution.py:8
  261.5 171.2 %all-gather.3.cloned.1.call-done = bf16[2048,4096]{1,0:T(8,128)(2,1)} async-done(((bf16[256,4096]{1,0:T(8,128)(2,1)}), bf16[2048,4096]{1,0:T(8,128)(2,1)}) %all-gather.3.cloned.1.call-update) | async-done | bytes 16777232 | tf_op jit(solution)/shard_map/all_gather | solution.py:53
  432.7 14.9 %fusion.7 = f32[2048,512]{1,0:T(8,128)} fusion(bf16[2048,4096]{1,0:T(8,128)(2,1)} %all-gather.3.cloned.1.call-done, bf16[1,512,4096]{2,1,0:T(8,128)(2,1)} %param.13), kind=kOutput, calls=%fused_computation.11 | convolution fusion | flops 8589934592 | bytes 25165824 | tf_op jit(solution)/shard_map/dot_general | solution.py:10
  447.6 30.3 %fusion = f32[2048,4096]{1,0:T(8,128)} fusion(bf16[1,4096,512]{2,1,0:T(8,128)(2,1)} %param.11, f32[2048,512]{1,0:T(8,128)} %fusion.2, f32[2048,512]{1,0:T(8,128)} %fusion.7, bf16[2048,4096]{1,0:T(8,128)(2,1)} %all-gather.5.cloned.1.call-done, bf16[1,4096,512]{2,1,0:T(8,128)(2,1)} %param.12), kind=kOutput, calls=%fused_computation.4 | convolution fusion | flops 17190354944 | bytes 67108864 | tf_op jit(solution)/shard_map/dot_general | solution.py:15
  477.9 25.7 %add_convert_fusion = bf16[2048,4096]{1,0:T(8,128)(2,1)} fusion(f32[2048,4096]{1,0:T(8,128)} %fusion, bf16[1,4096,512]{2,1,0:T(8,128)(2,1)} %param.12, f32[2048,512]{1,0:T(8,128)} %fusion.7, f32[2048,512]{1,0:T(8,128)} %fusion.2), kind=kOutput, calls=%fused_computation.3 | convolution fusion | flops 8613003264 | bytes 62914560 | tf_op jit(solution)/shard_map/dot_general | solution.py:15
  503.5 0.0 reduce-scatter.2.cloned.1.call-update
  503.6 191.9 %reduce-scatter.2.cloned.1.call-done = bf16[256,4096]{1,0:T(8,128)(2,1)} async-done(((bf16[2048,4096]{1,0:T(8,128)(2,1)}), bf16[256,4096]{1,0:T(8,128)(2,1)}) %reduce-scatter.2.cloned.1.call-update) | async-done | bytes 2097168 | tf_op jit(solution)/shard_map/reduce_scatter | solution.py:58
  695.4 5.8 all-to-all-start.2
  701.2 27.5 %all-to-all-done.2 = bf16[16,16,4096]{2,1,0:T(8,128)(2,1)S(1)} async-done(((bf16[16,16,4096]{2,1,0:T(8,128)(2,1)}), bf16[16,16,4096]{2,1,0:T(8,128)(2,1)S(1)}, u32[]{:S(2)}, u32[]{:S(2)}) %all-to-all-start.2) | async-done | bytes 2097184 | tf_op jit(solution)/shard_map/all_to_all | solution.py:64
  728.7 2.2 gather_fusion
  (1 shorter events, 0.0 us)
Async XLA Ops:
  6.5 240.0 %all-gather.5.cloned.1.call-start = ((), (), s32[]{:S(2)}) async-start(), calls=%async_computation.5 | async-start | bytes 18874368 | tf_op jit(solution)/shard_map/all_gather | solution.py:52
  9.0 35.6 %copy-start = (bf16[128,4096]{1,0:T(8,128)(2,1)S(1)}, bf16[128,4096]{1,0:T(8,128)(2,1)}, u32[]{:S(2)}) copy-start(bf16[128,4096]{1,0:T(8,128)(2,1)} %param.8) | copy-start | bytes 3145732
  9.0 35.6 %copy-start.1 = (f32[128]{0:T(128)S(1)}, f32[128]{0:T(128)}, u32[]{:S(2)}) copy-start(f32[128]{0:T(128)} %param.9) | copy-start | bytes 1540
  44.5 388.2 %all-gather.3.cloned.1.call-start = ((), (), s32[]{:S(2)}) async-start(), calls=%async_computation.4 | async-start | bytes 18874368 | tf_op jit(solution)/shard_map/all_gather | solution.py:53
  78.7 616.7 %reduce-scatter.2.cloned.1.call-start = ((), (), s32[]{:S(2)}) async-start(), calls=%async_computation.6 | async-start | bytes 18874368 | tf_op jit(solution)/shard_map/reduce_scatter | solution.py:58
  695.4 33.3 %all-to-all-start.2 = ((bf16[16,16,4096]{2,1,0:T(8,128)(2,1)}), bf16[16,16,4096]{2,1,0:T(8,128)(2,1)S(1)}, u32[]{:S(2)}, u32[]{:S(2)}) async-start(bf16[16,16,4096]{2,1,0:T(8,128)(2,1)} %bitcast.38), calls=%async_computation.3 | async-start | bytes 4194304 | tf_op jit(solution)/shard_map/all_to_all | solution.py:64
Sparse Core Ops, SparseCore 0:
  44.6 201.9 all-gather.4
  248.9 183.7 all-gather.2
  503.7 191.7 reduce-scatter.1
where the time goes:
time: 740 us; the launch traced here: 737 us
  waiting for transfers between devices  558 us (75%)
  matrix products  85.8 us (12%)
  blocking collectives  63.3 us (9%)
  between operations  13.2 us (2%)
    reduce_scatter x1, waiting for transfers between devices, shards(): lax.psum_scatter(expert_terms(group_x, group_grad, gate_local, up_local,...  192 us
    all_gather x1, waiting for transfers between devices, shards(): lax.all_gather(own_grads.reshape(-1, features), 'etp', axis=0, tiled=True)  171 us
    all_gather x1, waiting for transfers between devices, shards(): lax.all_gather(own_rows.reshape(-1, features), 'etp', axis=0, tiled=True)  168 us
    all_to_all x1, blocking collectives, shards(): lax.all_to_all(send_rows.reshape(experts, capacity, features), 'expert',...  32 us
    all_to_all x1, blocking collectives, shards(): lax.all_to_all(send_grads.reshape(experts, capacity, features), 'expert',...  31.3 us
    dot_general x1, matrix products, expert_terms(): jnp.dot(gate_grad, gate_local.T, preferred_element_type=jnp.float32)  30.3 us
    all_to_all x1, waiting for transfers between devices, shards(): lax.all_to_all(summed.reshape(experts, capacity, features), 'expert', spl...  27.5 us
    dot_general x1, matrix products, expert_terms(): jnp.dot(up_grad, up_local.T, preferred_element_type=jnp.float32)  25.7 us
  transfers between devices with their start and end apart: 4, of which 4 were waited for; matrix products, arithmetic and copies ran while one was open for 2% of the time, Pallas kernels for 0%

commit v1 on v0

v1 whole, which is shorter than its diff:
```python
import functools

import jax
import jax.numpy as jnp
from jax import lax
from jax.experimental import pallas as pl
from jax.experimental.pallas import tpu as pltpu
from jax.sharding import PartitionSpec as P

MESH = pl.DeviceIdType.MESH
BF16 = jnp.bfloat16
F32 = jnp.float32
D = 4096
UNITS = 512
CHUNKS = 4
SLOTS = 16
BLOCK = 4 * SLOTS
HALF = 4 * BLOCK
ROWS = 2 * HALF
EXPERTS = 16
COLS = 512
NT = (((1,), (1,)), ((), ()))


def mod4(value):
    return lax.rem(value + 8, 4)


def place(x, y, z, core):
    return (lax.rem(z, 2) * 4 + x) * 2 + core, y * 2 + z // 2


def kernel(
    tok, grad, prob, slot, w_gate, w_up, w_down,
    ret,
    rows, gate_v, up_v, down_v, send, land,
    a2a_s, a2a_r, ag_s, ag_r, fw_s, fw_r, sh_s, sh_r, w_s, w_r,
    sib_s, sib_r, half_s, half_r, full_s, full_r, ret_s, ret_r,
    cr_sib, cr_left, cr_right,
):
    e = lax.axis_index("expert")
    t = lax.axis_index("etp")
    core = lax.rem(e, 2)
    x = lax.rem(e // 2, 4)
    y = t // 2
    z_hi = lax.rem(t, 2)
    z = z_hi * 2 + e // 8
    other = 1 - core
    mine = (lax.rem(z, 2) * 4 + x) * 2 + z_hi
    y_right, y_left, y_far = mod4(y + 1), mod4(y - 1), mod4(y + 2)
    right, left = place(x, y_right, z, core), place(x, y_left, z, core)
    sibling = place(x, y, z, other)
    partner = place(x, y, mod4(z + 2), other)
    away = core != z_hi

    barrier = pltpu.get_barrier_semaphore()

    def greet(who):
        pl.semaphore_signal(barrier, inc=1, device_id=who, device_id_type=MESH)

    for k in range(1, 16):
        greet(place(mod4(x + k // 4), y, mod4(z + k % 4), core))
    for who in (right, left, sibling, partner):
        greet(who)

    onehot = (
        lax.broadcasted_iota(jnp.int32, (EXPERTS * SLOTS, tok.shape[0]), 0) == slot[...]
    ).astype(BF16)

    def fill(n, carry):
        cs = pl.ds(pl.multiple_of(n * COLS, COLS), COLS)
        send[0, :, cs] = jnp.dot(onehot, tok[:, cs], preferred_element_type=F32).astype(BF16)
        scaled = (prob[...] * grad[:, cs].astype(F32)).astype(BF16)
        send[1, :, cs] = jnp.dot(onehot, scaled, preferred_element_type=F32).astype(BF16)
        return carry

    lax.fori_loop(0, D // COLS, fill, 0)
    pl.semaphore_wait(barrier, 19)

    def remote(src, dst, s, r, who):
        return pltpu.make_async_remote_copy(
            src_ref=src, dst_ref=dst, send_sem=s, recv_sem=r, device_id=who, device_id_type=MESH
        )

    def rds(half, yo, off=0, n=BLOCK):
        return pl.ds(pl.multiple_of(half * HALF + yo * BLOCK + off, SLOTS), n)

    def a2a(j, dz):
        xd, zd = mod4(x + j + dz), mod4(z + dz)
        ed = (lax.rem(zd, 2) * 4 + xd) * 2 + zd // 2
        src = send.at[:, pl.ds(pl.multiple_of(ed * SLOTS, SLOTS), SLOTS), :]
        dst = rows.at[j, :, rds(core, y, dz * SLOTS, SLOTS), :]
        if j == 0 and dz == 0:
            return pltpu.make_async_copy(src, dst, a2a_r.at[0])
        return remote(src, dst, a2a_s.at[j * 4 + dz], a2a_r.at[j * 4 + dz], place(xd, y, zd, core))

    for j in range(CHUNKS):
        for dz in range(4):
            a2a(j, dz).start()

    def own(j, direction):
        ref = rows.at[j, :, rds(core, y), :]
        return remote(ref, ref, ag_s.at[j, direction], ag_r.at[j, direction], (right, left)[direction])

    def own_in(j, direction):
        ref = rows.at[j, :, rds(core, (y_left, y_right)[direction]), :]
        return remote(ref, ref, ag_s.at[j, direction], ag_r.at[j, direction], (right, left)[direction])

    def forward(j, direction):
        ref = rows.at[j, direction, rds(core, (y_left, y_right)[direction]), :]
        return remote(ref, ref, fw_s.at[j, direction], fw_r.at[j, direction], (right, left)[direction])

    def forward_in(j, direction):
        ref = rows.at[j, direction, rds(core, y_far), :]
        return remote(ref, ref, fw_s.at[j, direction], fw_r.at[j, direction], (right, left)[direction])

    def share(j, k, half):
        ref = rows.at[j, :, rds(half, mod4(y + k)), :]
        return remote(ref, ref, sh_s.at[j, k], sh_r.at[j, k], sibling)

    weights = ((w_gate, gate_v), (w_up, up_v), (w_down, down_v))

    def weight_in(k):
        return pltpu.make_async_copy(weights[k][0], weights[k][1], w_r.at[k])

    def weight_out(k):
        return remote(weights[k][0], weights[k][1], w_s.at[k], w_r.at[k], partner)

    def start_weights():
        @pl.when(away)
        def _():
            for k in range(3):
                weight_out(k).start()

        @pl.when(jnp.logical_not(away))
        def _():
            for k in range(3):
                weight_in(k).start()

    for j in range(CHUNKS):
        for dz in range(4):
            if j == 0 and dz == 0:
                a2a(j, dz).wait()
            else:
                a2a(j, dz).wait_recv()
        own(j, 0).start()
        own(j, 1).start()
        share(j, 0, core).start()
        if j == 1:
            start_weights()

    for j in range(CHUNKS):
        own_in(j, 0).wait_recv()
        forward(j, 0).start()
        share(j, 3, core).start()
        own_in(j, 1).wait_recv()
        forward(j, 1).start()
        share(j, 1, core).start()
        if j == 0:
            for k in range(1, 16):
                a2a(k // 4, k % 4).wait_send()
            pl.semaphore_signal(cr_sib, inc=2, device_id=sibling, device_id_type=MESH)

    for j in range(CHUNKS):
        forward_in(j, 0).wait_recv()
        forward_in(j, 1).wait_recv()
        share(j, 2, core).start()

    for j in range(CHUNKS):
        for direction in range(2):
            own(j, direction).wait_send()
            forward(j, direction).wait_send()
        for k in range(4):
            share(j, k, core).wait_send()
            share(j, k, other).wait_recv()

    @pl.when(away)
    def _():
        for k in range(3):
            weight_out(k).wait()

    @pl.when(jnp.logical_not(away))
    def _():
        for k in range(3):
            weight_in(k).wait()

    def compute(j, half):
        rs = pl.ds(pl.multiple_of(half * HALF, HALF), HALF)
        xr = rows[j, 0, rs, :]
        gate = jnp.dot(xr, gate_v[...], preferred_element_type=F32)
        up = jnp.dot(xr, up_v[...], preferred_element_type=F32)
        hidden = lax.dot_general(rows[j, 1, rs, :], down_v[...], NT, preferred_element_type=F32)
        sigma = jax.nn.sigmoid(gate)
        slope = sigma * (1.0 + gate * (1.0 - sigma))
        gate_grad = (hidden * up * slope).astype(BF16)
        up_grad = (hidden * gate * sigma).astype(BF16)

        def columns(n, carry):
            cs = pl.ds(pl.multiple_of(n * COLS, COLS), COLS)
            part = lax.dot_general(gate_grad, gate_v[cs, :], NT, preferred_element_type=F32)
            part += lax.dot_general(up_grad, up_v[cs, :], NT, preferred_element_type=F32)
            rows[j, 0, rs, cs] = part.astype(BF16)
            return carry

        lax.fori_loop(0, D // COLS, columns, 0)

    def add(j, at, n, sources):
        def body(k, carry):
            cs = pl.ds(pl.multiple_of(k * COLS, COLS), COLS)
            total = rows[j, 0, at, cs].astype(F32)
            for ref, first in sources:
                total += ref[pl.ds(first, n), cs].astype(F32)
            rows[j, 0, at, cs] = total.astype(BF16)
            return carry

        lax.fori_loop(0, D // COLS, body, 0)

    def sib(j, half):
        src = rows.at[j, 0, pl.ds(pl.multiple_of(half * HALF, HALF), HALF), :]
        return remote(src, send.at[lax.rem(j, 2)], sib_s.at[j], sib_r.at[j], sibling)

    def half_sum(j, direction):
        first = direction * (BLOCK // 2)
        src = rows.at[j, 0, rds(core, y_far, first, BLOCK // 2), :]
        dst = land.at[lax.rem(j, 2), pl.ds(first, BLOCK // 2), :]
        return remote(src, dst, half_s.at[j, direction], half_r.at[j, direction], (right, left)[direction])

    def full_sum(j, direction):
        src = rows.at[j, 0, rds(core, (y_right, y_left)[direction]), :]
        dst = land.at[lax.rem(j, 2), pl.ds(BLOCK * (1 + direction), BLOCK), :]
        return remote(src, dst, full_s.at[j, direction], full_r.at[j, direction], (right, left)[direction])

    def back(j, dz, run):
        xs, zs = mod4(x - j - dz), mod4(z - dz)
        src = rows.at[j, 0, rds(core, y, dz * SLOTS, SLOTS), :]
        dst = ret.at[pl.ds(pl.multiple_of(mine * SLOTS, SLOTS), SLOTS), :]
        copy = remote(src, dst, ret_s.at[j * 4 + dz], ret_r.at[j * 4 + dz], place(xs, y, zs, core))
        if dz:
            run(copy)
            return

        @pl.when(j > 0)
        def _():
            run(copy)

    def local_back():
        src = rows.at[0, 0, rds(core, y, 0, SLOTS), :]
        dst = ret.at[pl.ds(pl.multiple_of(mine * SLOTS, SLOTS), SLOTS), :]
        return pltpu.make_async_copy(src, dst, ret_r.at[0])

    def stage_sib(j):
        sib(j, other).wait_recv()
        add(j, pl.ds(pl.multiple_of(core * HALF, HALF), HALF), HALF, [(send.at[lax.rem(j, 2)], 0)])

        @pl.when(j < CHUNKS - 2)
        def _():
            pl.semaphore_signal(cr_sib, inc=1, device_id=sibling, device_id_type=MESH)

        @pl.when(j >= 2)
        def _():
            pl.semaphore_wait(cr_right, 1)
            pl.semaphore_wait(cr_left, 1)

        half_sum(j, 0).start()
        half_sum(j, 1).start()

    def stage_half(j):
        lands = land.at[lax.rem(j, 2)]
        half_sum(j, 0).wait_recv()
        add(j, rds(core, y_right, 0, BLOCK // 2), BLOCK // 2, [(lands, 0)])
        full_sum(j, 0).start()
        half_sum(j, 1).wait_recv()
        add(j, rds(core, y_left, BLOCK // 2, BLOCK // 2), BLOCK // 2, [(lands, BLOCK // 2)])
        full_sum(j, 1).start()

    def stage_full(j):
        lands = land.at[lax.rem(j, 2)]
        full_sum(j, 0).wait_recv()
        full_sum(j, 1).wait_recv()
        add(j, rds(core, y), BLOCK, [(lands, BLOCK), (lands, 2 * BLOCK)])

        @pl.when(j < CHUNKS - 2)
        def _():
            pl.semaphore_signal(cr_right, inc=1, device_id=left, device_id_type=MESH)
            pl.semaphore_signal(cr_left, inc=1, device_id=right, device_id_type=MESH)

        for dz in range(4):
            back(j, dz, lambda copy: copy.start())

        @pl.when(j == 0)
        def _():
            local_back().start()

    def step(j, carry):
        compute(j, other)
        pl.semaphore_wait(cr_sib, 1)
        sib(j, other).start()

        @pl.when(j >= 1)
        def _():
            stage_half(j - 1)

        @pl.when(j >= 2)
        def _():
            stage_full(j - 2)

        compute(j, core)
        stage_sib(j)
        return carry

    lax.fori_loop(0, CHUNKS, step, 0)
    stage_half(CHUNKS - 1)
    stage_full(CHUNKS - 2)
    stage_full(CHUNKS - 1)

    def finish(j, carry):
        sib(j, other).wait_send()
        for direction in range(2):
            half_sum(j, direction).wait_send()
            full_sum(j, direction).wait_send()
        for dz in range(4):
            back(j, dz, lambda copy: copy.wait())
        return carry

    lax.fori_loop(0, CHUNKS, finish, 0)
    local_back().wait()


def shards(tokens, grad_out, route_prob, expert_index, w_gate, w_up, w_down):
    expert_ids = expert_index[:, 0]
    chosen = (expert_ids[:, None] == jnp.arange(EXPERTS, dtype=jnp.int32)[None, :]).astype(jnp.int32)
    before = jnp.cumsum(chosen, axis=0) - chosen
    slot = expert_ids * SLOTS + jnp.sum(before * chosen, axis=1)
    vmem = pl.BlockSpec(memory_space=pltpu.VMEM)
    hbm = pl.BlockSpec(memory_space=pl.ANY)
    dma = pltpu.SemaphoreType.DMA
    regular = pltpu.SemaphoreType.REGULAR
    returned = pl.pallas_call(
        kernel,
        out_shape=jax.ShapeDtypeStruct((EXPERTS * SLOTS, D), BF16),
        in_specs=[vmem] * 4 + [hbm] * 3,
        out_specs=hbm,
        scratch_shapes=[
            pltpu.VMEM((CHUNKS, 2, ROWS, D), BF16),
            pltpu.VMEM((D, UNITS), BF16),
            pltpu.VMEM((D, UNITS), BF16),
            pltpu.VMEM((UNITS, D), BF16),
            pltpu.VMEM((2, HALF, D), BF16),
            pltpu.VMEM((2, 3 * BLOCK, D), BF16),
            dma((16,)), dma((16,)),
            dma((CHUNKS, 2)), dma((CHUNKS, 2)),
            dma((CHUNKS, 2)), dma((CHUNKS, 2)),
            dma((CHUNKS, 4)), dma((CHUNKS, 4)),
            dma((3,)), dma((3,)),
            dma((CHUNKS,)), dma((CHUNKS,)),
            dma((CHUNKS, 2)), dma((CHUNKS, 2)),
            dma((CHUNKS, 2)), dma((CHUNKS, 2)),
            dma((16,)), dma((16,)),
            regular, regular, regular,
        ],
        compiler_params=pltpu.CompilerParams(
            collective_id=1, has_side_effects=True, vmem_limit_bytes=63 * 1024 * 1024
        ),
        cost_estimate=pl.CostEstimate(
            flops=2 * CHUNKS * ROWS * D * UNITS * 5, bytes_accessed=64 << 20, transcendentals=0
        ),
    )(tokens, grad_out, route_prob[:, None], slot[None, :], w_gate[0], w_up[0], w_down[0])
    return returned[slot]


def solution(mesh):
    return jax.shard_map(
        shards,
        mesh=mesh,
        in_specs=(
            P(("expert", "etp"), None),
            P(("expert", "etp"), None),
            P(("expert", "etp")),
            P(("expert", "etp"), None),
            P("expert", None, "etp"),
            P("expert", None, "etp"),
            P("expert", "etp", None),
        ),
        out_specs=P(("expert", "etp"), None),
        check_vma=False,
    )
```

time: 740 us -> 298 us (0.40)
  waiting for transfers between devices: 558 us -> 0 us
  Pallas kernels: 0 us -> 284 us
  matrix products: 85.8 us -> 0 us
  blocking collectives: 63.3 us -> 0 us
  between operations: 13.2 us -> 0.02 us
    all_gather x2 -> x0, waiting for transfers between devices: 339 us -> none  [the longest x1 171 us: shards(): lax.all_gather(own_grads.reshape(-1, features), 'etp', axis=0, tiled=True)]
    pallas_call x0 -> x1, Pallas kernels: none -> 284 us  [shards(): pl.pallas_call(kernel, out_shape=jax.ShapeDtypeStruct((EXPERTS * SLOTS, D...]
    reduce_scatter x1 -> x0, waiting for transfers between devices: 192 us -> none  [shards(): lax.psum_scatter(expert_terms(group_x, group_grad, gate_local, up_local,...]
    dot_general x4 -> x0, matrix products: 85.8 us -> none  [the longest x1 30.3 us: expert_terms(): jnp.dot(gate_grad, gate_local.T, preferred_element_type=jnp.float32)]
    all_to_all x2 -> x0, blocking collectives: 63.3 us -> none  [the longest x1 32 us: shards(): lax.all_to_all(send_rows.reshape(experts, capacity, features), 'expert',...]
    all_to_all x1 -> x0, waiting for transfers between devices: 27.5 us -> none  [shards(): lax.all_to_all(summed.reshape(experts, capacity, features), 'expert', spl...]
  transfers between devices with their start and end apart: 4 -> 0, of which waited for: 4 -> 0; matrix products, arithmetic and copies ran while one was open for 2% -> 0% of each run, Pallas kernels for 0% -> 0%
where the time goes in v1:
time: 298 us; the launch traced here: 294 us
  Pallas kernels  284 us (95%)
  local copies, waits for them, and re-layouts  6.42 us (2%)
  other arithmetic  3.58 us (1%)
    pallas_call x1, Pallas kernels, shards(): pl.pallas_call(kernel, out_shape=jax.ShapeDtypeStruct((EXPERTS * SLOTS, D...  284 us

profile of v1, /device:TPU:96, one launch (start us, length us, event | category | flops | bytes accessed | tf_op | source)
XLA Modules:
  0.0 294.2 jit_solution(1540872115859747271)
XLA Ops:
  0.0 1.4 copy.8.prob
  1.4 0.7 fusion
  2.1 0.2 reduce_window_sum.11
  2.3 0.8 select_reduce_fusion
  3.1 0.7 fusion.1
  3.8 1.2 bitcast_add_fusion.1.slot
  5.0 284.1 %shard_map.73 = bf16[256,4096]{1,0:T(8,128)(2,1)} custom-call(bf16[128,4096]{1,0:T(8,128)(2,1)} %tok.1, bf16[128,4096]{1,0:T(8,128)(2,1)} %grad.1, f32[128,1]{1,0:T(8,128)} %copy.8.prob, s32[1,128]{1,0:T(1,128)} %bitcast_add_fusion.1.slot, bf16[4096,512]{1,0:T(8,128)(2,1)} %bitcast.18, bf16[4096,512]{1,0:T(8,128)(2,1)} %bitcast.19, bf16[512,4096]{1,0:T(8,128)(2,1)} %bitcast.20), custom_call_target="tpu_custom_call" | custom-call | flops 42949672960 | bytes 67108864 | tf_op jit(solution)/shard_map/pallas_call | solution.py:338
  289.1 5.0 %gather_fusion = bf16[128,4096]{1,0:T(8,128)(2,1)} fusion(bf16[256,4096]{1,0:T(8,128)(2,1)} %shard_map.73, s32[1024]{0:T(1024)S(1)} %pad_clamp_fusion), kind=kCustom, calls=%fused_computation | custom fusion | bytes 2097664 | tf_op jit(solution)/shard_map/gather | solution.py:368
  (1 shorter events, 0.0 us)

commit v2 on v1

v2 whole, which is shorter than its diff:
```python
import functools

import jax
import jax.numpy as jnp
from jax import lax
from jax.experimental import pallas as pl
from jax.experimental.pallas import tpu as pltpu
from jax.sharding import PartitionSpec as P

MESH = pl.DeviceIdType.MESH
BF16 = jnp.bfloat16
F32 = jnp.float32
D = 4096
UNITS = 512
CHUNKS = 4
SLOTS = 16
BLOCK = 4 * SLOTS
HALF = 4 * BLOCK
ROWS = 2 * HALF
EXPERTS = 16
COLS = 512
PART = UNITS // 2
WIDE = D // 2
NT = (((1,), (1,)), ((), ()))


def mod4(value):
    return lax.rem(value + 8, 4)


def place(x, y, z, core):
    return (lax.rem(z, 2) * 4 + x) * 2 + core, y * 2 + z // 2


def kernel(
    tok, grad, prob, index, w_gate, w_up, w_down,
    out,
    rows, gate_v, up_v, down_v, send, land, ret, gate_t, up_t, onehot_t,
    a2a_s, a2a_r, ag_s, ag_r, fw_s, fw_r, sh_s, sh_r, w_s, w_r,
    sib_s, sib_r, half_s, half_r, full_s, full_r, ret_s, ret_r,
    cr_sib, cr_left, cr_right,
):
    e = lax.axis_index("expert")
    t = lax.axis_index("etp")
    core = lax.rem(e, 2)
    x = lax.rem(e // 2, 4)
    y = t // 2
    z_hi = lax.rem(t, 2)
    z = z_hi * 2 + e // 8
    other = 1 - core
    mine = (lax.rem(z, 2) * 4 + x) * 2 + z_hi
    y_right, y_left, y_far = mod4(y + 1), mod4(y - 1), mod4(y + 2)
    right, left = place(x, y_right, z, core), place(x, y_left, z, core)
    sibling = place(x, y, z, other)
    partner = place(x, y, mod4(z + 2), other)
    away = core != z_hi

    barrier = pltpu.get_barrier_semaphore()

    def greet(who):
        pl.semaphore_signal(barrier, inc=1, device_id=who, device_id_type=MESH)

    for k in range(1, 16):
        greet(place(mod4(x + k // 4), y, mod4(z + k % 4), core))
    for who in (right, left, sibling, partner):
        greet(who)

    n_tok = tok.shape[0]
    at_row = lax.broadcasted_iota(jnp.int32, (n_tok, n_tok), 0)
    at_col = lax.broadcasted_iota(jnp.int32, (n_tok, n_tok), 1)
    earlier = (at_row < at_col).astype(BF16)
    same = (at_row == at_col).astype(F32)
    ids = index[...]
    chosen = (lax.broadcasted_iota(jnp.int32, (EXPERTS, n_tok), 0) == ids).astype(F32)
    before = jnp.dot(chosen.astype(BF16), earlier, preferred_element_type=F32)
    slot = ids.astype(F32) * SLOTS + jnp.sum(before * chosen, axis=0, keepdims=True)
    slot_col = jnp.sum(same * slot, axis=1, keepdims=True)
    scale = jnp.sum(same * prob[...], axis=1, keepdims=True)
    n_slot = EXPERTS * SLOTS
    onehot = (lax.broadcasted_iota(jnp.int32, (n_slot, n_tok), 0).astype(F32) == slot).astype(BF16)
    onehot_t[...] = (
        lax.broadcasted_iota(jnp.int32, (n_tok, n_slot), 1).astype(F32) == slot_col
    ).astype(BF16)

    def fill(n, carry):
        cs = pl.ds(pl.multiple_of(n * COLS, COLS), COLS)
        send[0, :, cs] = jnp.dot(onehot, tok[:, cs], preferred_element_type=F32).astype(BF16)
        scaled = (scale * grad[:, cs].astype(F32)).astype(BF16)
        send[1, :, cs] = jnp.dot(onehot, scaled, preferred_element_type=F32).astype(BF16)
        return carry

    lax.fori_loop(0, D // COLS, fill, 0)
    pl.semaphore_wait(barrier, 19)

    def remote(src, dst, s, r, who):
        return pltpu.make_async_remote_copy(
            src_ref=src, dst_ref=dst, send_sem=s, recv_sem=r, device_id=who, device_id_type=MESH
        )

    def rds(half, yo, off=0, n=BLOCK):
        return pl.ds(pl.multiple_of(half * HALF + yo * BLOCK + off, SLOTS), n)

    def a2a(j, dz):
        xd, zd = mod4(x + j + dz), mod4(z + dz)
        ed = (lax.rem(zd, 2) * 4 + xd) * 2 + zd // 2
        src = send.at[:, pl.ds(pl.multiple_of(ed * SLOTS, SLOTS), SLOTS), :]
        dst = rows.at[j, :, rds(core, y, dz * SLOTS, SLOTS), :]
        if j == 0 and dz == 0:
            return pltpu.make_async_copy(src, dst, a2a_r.at[0])
        return remote(src, dst, a2a_s.at[j * 4 + dz], a2a_r.at[j * 4 + dz], place(xd, y, zd, core))

    for j in range(CHUNKS):
        for dz in range(4):
            a2a(j, dz).start()

    def own(j, direction):
        ref = rows.at[j, :, rds(core, y), :]
        return remote(ref, ref, ag_s.at[j, direction], ag_r.at[j, direction], (right, left)[direction])

    def own_in(j, direction):
        ref = rows.at[j, :, rds(core, (y_left, y_right)[direction]), :]
        return remote(ref, ref, ag_s.at[j, direction], ag_r.at[j, direction], (right, left)[direction])

    def forward(j, direction):
        ref = rows.at[j, direction, rds(core, (y_left, y_right)[direction]), :]
        return remote(ref, ref, fw_s.at[j, direction], fw_r.at[j, direction], (right, left)[direction])

    def forward_in(j, direction):
        ref = rows.at[j, direction, rds(core, y_far), :]
        return remote(ref, ref, fw_s.at[j, direction], fw_r.at[j, direction], (right, left)[direction])

    def share(j, k, half):
        ref = rows.at[j, :, rds(half, mod4(y + k)), :]
        return remote(ref, ref, sh_s.at[j, k], sh_r.at[j, k], sibling)

    def weight_refs(p, k):
        units = pl.ds(p * PART, PART)
        return (
            (w_gate.at[:, units], gate_v.at[p]),
            (w_up.at[:, units], up_v.at[p]),
            (w_down.at[units, :], down_v.at[p]),
        )[k]

    def weight_in(p, k):
        src, dst = weight_refs(p, k)
        return pltpu.make_async_copy(src, dst, w_r.at[p, k])

    def weight_out(p, k):
        src, dst = weight_refs(p, k)
        return remote(src, dst, w_s.at[p, k], w_r.at[p, k], partner)

    def start_weights(p):
        @pl.when(away)
        def _():
            for k in range(3):
                weight_out(p, k).start()

        @pl.when(jnp.logical_not(away))
        def _():
            for k in range(3):
                weight_in(p, k).start()

    def wait_weights(p):
        @pl.when(away)
        def _():
            for k in range(3):
                weight_out(p, k).wait()

        @pl.when(jnp.logical_not(away))
        def _():
            for k in range(3):
                weight_in(p, k).wait()

    for j in range(CHUNKS):
        for dz in range(4):
            if j == 0 and dz == 0:
                a2a(j, dz).wait()
            else:
                a2a(j, dz).wait_recv()
        own(j, 0).start()
        own(j, 1).start()
        share(j, 0, core).start()
        if j == 1:
            start_weights(0)

    for j in range(CHUNKS):
        own_in(j, 0).wait_recv()
        forward(j, 0).start()
        share(j, 3, core).start()
        own_in(j, 1).wait_recv()
        forward(j, 1).start()
        share(j, 1, core).start()
        if j == 1:
            start_weights(1)
        if j == 0:
            for k in range(1, 16):
                a2a(k // 4, k % 4).wait_send()
            pl.semaphore_signal(cr_sib, inc=2, device_id=sibling, device_id_type=MESH)

    for j in range(CHUNKS):
        forward_in(j, 0).wait_recv()
        forward_in(j, 1).wait_recv()
        share(j, 2, core).start()

    for j in range(CHUNKS):
        for direction in range(2):
            own(j, direction).wait_send()
            forward(j, direction).wait_send()
        for k in range(4):
            share(j, k, core).wait_send()
            share(j, k, other).wait_recv()

    def half_rows(half):
        return pl.ds(pl.multiple_of(half * HALF, HALF), HALF)

    def terms(j, half, p):
        rs = half_rows(half)
        xr = rows[j, 0, rs, :]
        gate = jnp.dot(xr, gate_v[p], preferred_element_type=F32)
        up = jnp.dot(xr, up_v[p], preferred_element_type=F32)
        hidden = lax.dot_general(rows[j, 1, rs, :], down_v[p], NT, preferred_element_type=F32)
        sigma = jax.nn.sigmoid(gate)
        slope = sigma * (1.0 + gate * (1.0 - sigma))
        return (hidden * up * slope).astype(BF16), (hidden * gate * sigma).astype(BF16)

    def products(j, half, last, ch, received):
        rs = half_rows(half)
        gate_last, up_last = last

        def columns(n, carry):
            cs = pl.ds(pl.multiple_of(ch * WIDE + n * COLS, COLS), COLS)
            part = lax.dot_general(gate_t[j, rs, :], gate_v[0, cs, :], NT, preferred_element_type=F32)
            part += lax.dot_general(up_t[j, rs, :], up_v[0, cs, :], NT, preferred_element_type=F32)
            part += lax.dot_general(gate_last, gate_v[1, cs, :], NT, preferred_element_type=F32)
            part += lax.dot_general(up_last, up_v[1, cs, :], NT, preferred_element_type=F32)
            if received:
                part += send[lax.rem(j, 2), :, cs].astype(F32)
            rows[j, 0, rs, cs] = part.astype(BF16)
            return carry

        lax.fori_loop(0, WIDE // COLS, columns, 0)

    def add(j, at, n, ch, sources):
        def body(k, carry):
            cs = pl.ds(pl.multiple_of(ch * WIDE + k * COLS, COLS), COLS)
            total = rows[j, 0, at, cs].astype(F32)
            for first in sources:
                total += land[lax.rem(j, 2), pl.ds(first, n), cs].astype(F32)
            rows[j, 0, at, cs] = total.astype(BF16)
            return carry

        lax.fori_loop(0, WIDE // COLS, body, 0)

    def wide(ch):
        return pl.ds(ch * WIDE, WIDE)

    def sib(j, ch):
        src = rows.at[j, 0, half_rows(other), wide(ch)]
        dst = send.at[lax.rem(j, 2), :, wide(ch)]
        return remote(src, dst, sib_s.at[j, ch], sib_r.at[j, ch], sibling)

    def half_sum(j, ch, direction):
        first = direction * (BLOCK // 2)
        src = rows.at[j, 0, rds(core, y_far, first, BLOCK // 2), wide(ch)]
        dst = land.at[lax.rem(j, 2), pl.ds(first, BLOCK // 2), wide(ch)]
        k = 2 * ch + direction
        return remote(src, dst, half_s.at[j, k], half_r.at[j, k], (right, left)[direction])

    def full_sum(j, ch, direction):
        src = rows.at[j, 0, rds(core, (y_right, y_left)[direction]), wide(ch)]
        dst = land.at[lax.rem(j, 2), pl.ds(BLOCK * (1 + direction), BLOCK), wide(ch)]
        k = 2 * ch + direction
        return remote(src, dst, full_s.at[j, k], full_r.at[j, k], (right, left)[direction])

    def back_refs(j, ch, dz):
        src = rows.at[j, 0, rds(core, y, dz * SLOTS, SLOTS), wide(ch)]
        dst = ret.at[pl.ds(pl.multiple_of(mine * SLOTS, SLOTS), SLOTS), wide(ch)]
        return src, dst

    def back(j, ch, dz):
        src, dst = back_refs(j, ch, dz)
        who = place(mod4(x - j - dz), y, mod4(z - dz), core)
        return remote(src, dst, ret_s.at[j * 4 + dz, ch], ret_r.at[j * 4 + dz, ch], who)

    def local_back(ch):
        src, dst = back_refs(0, ch, 0)
        return pltpu.make_async_copy(src, dst, ret_r.at[0, ch])

    def stage_half(j, ch):
        half_sum(j, ch, 0).wait_recv()
        add(j, rds(core, y_right, 0, BLOCK // 2), BLOCK // 2, ch, [0])
        full_sum(j, ch, 0).start()
        half_sum(j, ch, 1).wait_recv()
        add(j, rds(core, y_left, BLOCK // 2, BLOCK // 2), BLOCK // 2, ch, [BLOCK // 2])
        full_sum(j, ch, 1).start()

    def stage_full(j, ch):
        full_sum(j, ch, 0).wait_recv()
        full_sum(j, ch, 1).wait_recv()
        add(j, rds(core, y), BLOCK, ch, [BLOCK, 2 * BLOCK])
        for dz in range(1, 4):
            back(j, ch, dz).start()

        @pl.when(j > 0)
        def _():
            back(j, ch, 0).start()

        @pl.when(j == 0)
        def _():
            local_back(ch).start()

    def credit(j):
        @pl.when(j < CHUNKS - 2)
        def _():
            pl.semaphore_signal(cr_right, inc=1, device_id=left, device_id_type=MESH)
            pl.semaphore_signal(cr_left, inc=1, device_id=right, device_id_type=MESH)

    wait_weights(0)

    def early(j, carry):
        for half in (other, core):
            gate_part, up_part = terms(j, half, 0)
            gate_t[j, half_rows(half), :] = gate_part
            up_t[j, half_rows(half), :] = up_part
        return carry

    lax.fori_loop(0, CHUNKS, early, 0)
    wait_weights(1)

    def step(j, carry):
        last = terms(j, other, 1)
        pl.semaphore_wait(cr_sib, 1)
        for ch in range(2):
            products(j, other, last, ch, False)
            sib(j, ch).start()

        @pl.when(j >= 1)
        def _():
            stage_half(j - 1, 1)

        last = terms(j, core, 1)

        @pl.when(j >= 1)
        def _():
            stage_full(j - 1, 0)

        @pl.when(j >= 2)
        def _():
            pl.semaphore_wait(cr_right, 1)
            pl.semaphore_wait(cr_left, 1)

        for ch in range(2):
            sib(j, ch).wait_recv()
            products(j, core, last, ch, True)
            half_sum(j, ch, 0).start()
            half_sum(j, ch, 1).start()

        @pl.when(j < CHUNKS - 2)
        def _():
            pl.semaphore_signal(cr_sib, inc=1, device_id=sibling, device_id_type=MESH)

        @pl.when(j >= 1)
        def _():
            stage_full(j - 1, 1)
            credit(j - 1)

        stage_half(j, 0)
        return carry

    lax.fori_loop(0, CHUNKS, step, 0)
    stage_half(CHUNKS - 1, 1)
    stage_full(CHUNKS - 1, 0)
    stage_full(CHUNKS - 1, 1)

    for ch in range(2):
        local_back(ch).wait()
        for k in range(1, 16):
            back(k // 4, ch, k % 4).wait_recv()

        def pick(n, carry):
            cs = pl.ds(pl.multiple_of(ch * WIDE + n * COLS, COLS), COLS)
            out[:, cs] = jnp.dot(onehot_t[...], ret[:, cs], preferred_element_type=F32).astype(BF16)
            return carry

        lax.fori_loop(0, WIDE // COLS, pick, 0)

    for ch in range(2):
        for k in range(1, 16):
            back(k // 4, ch, k % 4).wait_send()

    def finish(j, carry):
        for ch in range(2):
            sib(j, ch).wait_send()
            for direction in range(2):
                half_sum(j, ch, direction).wait_send()
                full_sum(j, ch, direction).wait_send()
        return carry

    lax.fori_loop(0, CHUNKS, finish, 0)


def shards(tokens, grad_out, route_prob, expert_index, w_gate, w_up, w_down):
    vmem = pl.BlockSpec(memory_space=pltpu.VMEM)
    hbm = pl.BlockSpec(memory_space=pl.ANY)
    dma = pltpu.SemaphoreType.DMA
    regular = pltpu.SemaphoreType.REGULAR
    n_tok = tokens.shape[0]
    return pl.pallas_call(
        kernel,
        out_shape=jax.ShapeDtypeStruct((n_tok, D), BF16),
        in_specs=[vmem] * 4 + [hbm] * 3,
        out_specs=vmem,
        scratch_shapes=[
            pltpu.VMEM((CHUNKS, 2, ROWS, D), BF16),
            pltpu.VMEM((2, D, PART), BF16),
            pltpu.VMEM((2, D, PART), BF16),
            pltpu.VMEM((2, PART, D), BF16),
            pltpu.VMEM((2, HALF, D), BF16),
            pltpu.VMEM((2, 3 * BLOCK, D), BF16),
            pltpu.VMEM((EXPERTS * SLOTS, D), BF16),
            pltpu.VMEM((CHUNKS, ROWS, PART), BF16),
            pltpu.VMEM((CHUNKS, ROWS, PART), BF16),
            pltpu.VMEM((n_tok, EXPERTS * SLOTS), BF16),
            dma((16,)), dma((16,)),
            dma((CHUNKS, 2)), dma((CHUNKS, 2)),
            dma((CHUNKS, 2)), dma((CHUNKS, 2)),
            dma((CHUNKS, 4)), dma((CHUNKS, 4)),
            dma((2, 3)), dma((2, 3)),
            dma((CHUNKS, 2)), dma((CHUNKS, 2)),
            dma((CHUNKS, 4)), dma((CHUNKS, 4)),
            dma((CHUNKS, 4)), dma((CHUNKS, 4)),
            dma((16, 2)), dma((16, 2)),
            regular, regular, regular,
        ],
        compiler_params=pltpu.CompilerParams(
            collective_id=1, has_side_effects=True, vmem_limit_bytes=63 * 1024 * 1024
        ),
        cost_estimate=pl.CostEstimate(
            flops=2 * CHUNKS * ROWS * D * UNITS * 5, bytes_accessed=64 << 20, transcendentals=0
        ),
    )(
        tokens, grad_out, route_prob.reshape(1, n_tok), expert_index.reshape(1, n_tok),
        w_gate[0], w_up[0], w_down[0],
    )


def solution(mesh):
    return jax.shard_map(
        shards,
        mesh=mesh,
        in_specs=(
            P(("expert", "etp"), None),
            P(("expert", "etp"), None),
            P(("expert", "etp")),
            P(("expert", "etp"), None),
            P("expert", None, "etp"),
            P("expert", None, "etp"),
            P("expert", "etp", None),
        ),
        out_specs=P(("expert", "etp"), None),
        check_vma=False,
    )
```

time: 298 us -> 286 us (0.960)
  local copies, waits for them, and re-layouts: 6.42 us -> 2.29 us
  Pallas kernels: 284 us -> 280 us
  other arithmetic: 3.58 us -> 0 us
    gather x1 -> x0, local copies, waits for them, and re-layouts: 5.04 us -> none  [shards(): return returned[slot]]
    pallas_call x1, Pallas kernels: 284 us -> 280 us  [shards(): pl.pallas_call(kernel, out_shape=jax.ShapeDtypeStruct((n_tok, D), BF16),...]
where the time goes in v2:
time: 286 us; the launch traced here: 282 us
  Pallas kernels  280 us (98%)
    pallas_call x1, Pallas kernels, shards(): pl.pallas_call(kernel, out_shape=jax.ShapeDtypeStruct((n_tok, D), BF16),...  280 us

profile of v2, /device:TPU:96, one launch (start us, length us, event | category | flops | bytes accessed | tf_op | source)
XLA Modules:
  0.0 282.3 jit_solution(17149883434938794064)
XLA Ops:
  0.0 280.0 %shard_map.73 = bf16[128,4096]{1,0:T(8,128)(2,1)} custom-call(bf16[128,4096]{1,0:T(8,128)(2,1)} %tok.1, bf16[128,4096]{1,0:T(8,128)(2,1)} %grad.1, f32[1,128]{1,0:T(1,128)} %bitcast.8, s32[1,128]{1,0:T(1,128)} %bitcast.9, bf16[4096,512]{1,0:T(8,128)(2,1)} %bitcast.5, bf16[4096,512]{1,0:T(8,128)(2,1)} %bitcast.6, bf16[512,4096]{1,0:T(8,128)(2,1)} %bitcast.7), custom_call_target="tpu_custom_call" | custom-call | flops 42949672960 | bytes 67108864 | tf_op jit(solution)/shard_map/pallas_call | solution.py:408
  280.0 2.3 copy.9

commit v3 on v2

--- a/solution.py
+++ b/solution.py
@@ -19,8 +19,15 @@
 ROWS = 2 * HALF
 EXPERTS = 16
 COLS = 512
-PART = UNITS // 2
-WIDE = D // 2
+PIECES = ((0, 384), (384, 128))
+WIDTHS = 4
+WIDE = D // WIDTHS
+STEPS = (
+    ((0, 0), (1, 1), (2, 2), (3, 3)),
+    ((1, 0), (2, 1), (3, 2), (0, 3)),
+    ((2, 0), (3, 1), (0, 2), (1, 3)),
+    ((3, 0), (0, 1), (1, 2), (2, 3)),
+)
 NT = (((1,), (1,)), ((), ()))
 
 
@@ -28,14 +35,24 @@
     return lax.rem(value + 8, 4)
 
 
+def step_of(j, k):
+    if isinstance(j, int):
+        return STEPS[j][k]
+    dx, dz = STEPS[0][k]
+    for t in range(1, CHUNKS):
+        dx = jnp.where(j == t, STEPS[t][k][0], dx)
+        dz = jnp.where(j == t, STEPS[t][k][1], dz)
+    return dx, dz
+
+
 def place(x, y, z, core):
     return (lax.rem(z, 2) * 4 + x) * 2 + core, y * 2 + z // 2
 
 
 def kernel(
-    tok, grad, prob, index, w_gate, w_up, w_down,
+    tok_h, grad_h, prob, index, w_gate, w_up, w_down,
     out,
-    rows, gate_v, up_v, down_v, send, land, ret, gate_t, up_t, onehot_t,
+    rows, gu_v, down_v, send, ret, terms_v, onehot_t, tok, grad, in_s,
     a2a_s, a2a_r, ag_s, ag_r, fw_s, fw_r, sh_s, sh_r, w_s, w_r,
     sib_s, sib_r, half_s, half_r, full_s, full_r, ret_s, ret_r,
     cr_sib, cr_left, cr_right,
@@ -55,6 +72,11 @@
     partner = place(x, y, mod4(z + 2), other)
     away = core != z_hi
 
+    tok_in = pltpu.make_async_copy(tok_h, tok, in_s.at[0])
+    grad_in = pltpu.make_async_copy(grad_h, grad, in_s.at[1])
+    tok_in.start()
+    grad_in.start()
+
     barrier = pltpu.get_barrier_semaphore()
 
     def greet(who):
@@ -89,6 +111,8 @@
         send[1, :, cs] = jnp.dot(onehot, scaled, preferred_element_type=F32).astype(BF16)
         return carry
 
+    tok_in.wait()
+    grad_in.wait()
     lax.fori_loop(0, D // COLS, fill, 0)
     pl.semaphore_wait(barrier, 19)
 
@@ -100,18 +124,19 @@
     def rds(half, yo, off=0, n=BLOCK):
         return pl.ds(pl.multiple_of(half * HALF + yo * BLOCK + off, SLOTS), n)
 
-    def a2a(j, dz):
-        xd, zd = mod4(x + j + dz), mod4(z + dz)
+    def a2a(j, k):
+        dx, dz = step_of(j, k)
+        xd, zd = mod4(x + dx), mod4(z + dz)
         ed = (lax.rem(zd, 2) * 4 + xd) * 2 + zd // 2
         src = send.at[:, pl.ds(pl.multiple_of(ed * SLOTS, SLOTS), SLOTS), :]
-        dst = rows.at[j, :, rds(core, y, dz * SLOTS, SLOTS), :]
-        if j == 0 and dz == 0:
+        dst = rows.at[j, :, rds(core, y, k * SLOTS, SLOTS), :]
+        if j == 0 and k == 0:
             return pltpu.make_async_copy(src, dst, a2a_r.at[0])
-        return remote(src, dst, a2a_s.at[j * 4 + dz], a2a_r.at[j * 4 + dz], place(xd, y, zd, core))
+        return remote(src, dst, a2a_s.at[j * 4 + k], a2a_r.at[j * 4 + k], place(xd, y, zd, core))
 
     for j in range(CHUNKS):
-        for dz in range(4):
-            a2a(j, dz).start()
+        for k in range(4):
+            a2a(j, k).start()
 
     def own(j, direction):
         ref = rows.at[j, :, rds(core, y), :]
@@ -134,11 +159,12 @@
         return remote(ref, ref, sh_s.at[j, k], sh_r.at[j, k], sibling)
 
     def weight_refs(p, k):
-        units = pl.ds(p * PART, PART)
+        first, n = PIECES[p]
+        units = pl.ds(first, n)
         return (
-            (w_gate.at[:, units], gate_v.at[p]),
-            (w_up.at[:, units], up_v.at[p]),
-            (w_down.at[units, :], down_v.at[p]),
+            (w_gate.at[:, units], gu_v.at[:, pl.ds(2 * first, n)]),
+            (w_up.at[:, units], gu_v.at[:, pl.ds(2 * first + n, n)]),
+            (w_down.at[units, :], down_v.at[units, :]),
         )[k]
 
     def weight_in(p, k):
@@ -172,11 +198,11 @@
                 weight_in(p, k).wait()
 
     for j in range(CHUNKS):
-        for dz in range(4):
-            if j == 0 and dz == 0:
-                a2a(j, dz).wait()
+        for k in range(4):
+            if j == 0 and k == 0:
+                a2a(j, k).wait()
             else:
-                a2a(j, dz).wait_recv()
+                a2a(j, k).wait_recv()
         own(j, 0).start()
         own(j, 1).start()
         share(j, 0, core).start()
@@ -192,60 +218,47 @@
         share(j, 1, core).start()
         if j == 1:
             start_weights(1)
-        if j == 0:
-            for k in range(1, 16):
-                a2a(k // 4, k % 4).wait_send()
-            pl.semaphore_signal(cr_sib, inc=2, device_id=sibling, device_id_type=MESH)
-
-    for j in range(CHUNKS):
-        forward_in(j, 0).wait_recv()
-        forward_in(j, 1).wait_recv()
-        share(j, 2, core).start()
-
-    for j in range(CHUNKS):
-        for direction in range(2):
-            own(j, direction).wait_send()
-            forward(j, direction).wait_send()
-        for k in range(4):
-            share(j, k, core).wait_send()
-            share(j, k, other).wait_recv()
 
     def half_rows(half):
         return pl.ds(pl.multiple_of(half * HALF, HALF), HALF)
 
     def terms(j, half, p):
         rs = half_rows(half)
-        xr = rows[j, 0, rs, :]
-        gate = jnp.dot(xr, gate_v[p], preferred_element_type=F32)
-        up = jnp.dot(xr, up_v[p], preferred_element_type=F32)
-        hidden = lax.dot_general(rows[j, 1, rs, :], down_v[p], NT, preferred_element_type=F32)
+        first, n = PIECES[p]
+        both = jnp.dot(
+            rows[j, 0, rs, :], gu_v[:, 2 * first : 2 * (first + n)], preferred_element_type=F32
+        )
+        gate, up = both[:, :n], both[:, n:]
+        hidden = lax.dot_general(
+            rows[j, 1, rs, :], down_v[first : first + n, :], NT, preferred_element_type=F32
+        )
         sigma = jax.nn.sigmoid(gate)
         slope = sigma * (1.0 + gate * (1.0 - sigma))
-        return (hidden * up * slope).astype(BF16), (hidden * gate * sigma).astype(BF16)
-
-    def products(j, half, last, ch, received):
+        terms_v[j, rs, 2 * first : 2 * first + n] = (hidden * up * slope).astype(BF16)
+        terms_v[j, rs, 2 * first + n : 2 * (first + n)] = (hidden * gate * sigma).astype(BF16)
+
+    def products(j, half, ch, received):
         rs = half_rows(half)
-        gate_last, up_last = last
 
         def columns(n, carry):
             cs = pl.ds(pl.multiple_of(ch * WIDE + n * COLS, COLS), COLS)
-            part = lax.dot_general(gate_t[j, rs, :], gate_v[0, cs, :], NT, preferred_element_type=F32)
-            part += lax.dot_general(up_t[j, rs, :], up_v[0, cs, :], NT, preferred_element_type=F32)
-            part += lax.dot_general(gate_last, gate_v[1, cs, :], NT, preferred_element_type=F32)
-            part += lax.dot_general(up_last, up_v[1, cs, :], NT, preferred_element_type=F32)
+            part = lax.dot_general(terms_v[j, rs, :], gu_v[cs, :], NT, preferred_element_type=F32)
             if received:
-                part += send[lax.rem(j, 2), :, cs].astype(F32)
+                part += rows[j, 1, half_rows(other), cs].astype(F32)
             rows[j, 0, rs, cs] = part.astype(BF16)
             return carry
 
         lax.fori_loop(0, WIDE // COLS, columns, 0)
+
+    def landing(first, n):
+        return pl.ds(pl.multiple_of(core * HALF + first, BLOCK // 2), n)
 
     def add(j, at, n, ch, sources):
         def body(k, carry):
             cs = pl.ds(pl.multiple_of(ch * WIDE + k * COLS, COLS), COLS)
             total = rows[j, 0, at, cs].astype(F32)
             for first in sources:
-                total += land[lax.rem(j, 2), pl.ds(first, n), cs].astype(F32)
+                total += rows[j, 1, landing(first, n), cs].astype(F32)
             rows[j, 0, at, cs] = total.astype(BF16)
             return carry
 
@@ -256,31 +269,32 @@
 
     def sib(j, ch):
         src = rows.at[j, 0, half_rows(other), wide(ch)]
-        dst = send.at[lax.rem(j, 2), :, wide(ch)]
+        dst = rows.at[j, 1, half_rows(core), wide(ch)]
         return remote(src, dst, sib_s.at[j, ch], sib_r.at[j, ch], sibling)
 
     def half_sum(j, ch, direction):
         first = direction * (BLOCK // 2)
         src = rows.at[j, 0, rds(core, y_far, first, BLOCK // 2), wide(ch)]
-        dst = land.at[lax.rem(j, 2), pl.ds(first, BLOCK // 2), wide(ch)]
+        dst = rows.at[j, 1, landing(first, BLOCK // 2), wide(ch)]
         k = 2 * ch + direction
         return remote(src, dst, half_s.at[j, k], half_r.at[j, k], (right, left)[direction])
 
     def full_sum(j, ch, direction):
         src = rows.at[j, 0, rds(core, (y_right, y_left)[direction]), wide(ch)]
-        dst = land.at[lax.rem(j, 2), pl.ds(BLOCK * (1 + direction), BLOCK), wide(ch)]
+        dst = rows.at[j, 1, landing(BLOCK * (1 + direction), BLOCK), wide(ch)]
         k = 2 * ch + direction
         return remote(src, dst, full_s.at[j, k], full_r.at[j, k], (right, left)[direction])
 
-    def back_refs(j, ch, dz):
-        src = rows.at[j, 0, rds(core, y, dz * SLOTS, SLOTS), wide(ch)]
+    def back_refs(j, ch, k):
+        src = rows.at[j, 0, rds(core, y, k * SLOTS, SLOTS), wide(ch)]
         dst = ret.at[pl.ds(pl.multiple_of(mine * SLOTS, SLOTS), SLOTS), wide(ch)]
         return src, dst
 
-    def back(j, ch, dz):
-        src, dst = back_refs(j, ch, dz)
-        who = place(mod4(x - j - dz), y, mod4(z - dz), core)
-        return remote(src, dst, ret_s.at[j * 4 + dz, ch], ret_r.at[j * 4 + dz, ch], who)
+    def back(j, ch, k):
+        src, dst = back_refs(j, ch, k)
+        dx, dz = step_of(j, k)
+        who = place(mod4(x - dx), y, mod4(z - dz), core)
+        return remote(src, dst, ret_s.at[j * 4 + k, ch], ret_r.at[j * 4 + k, ch], who)
 
     def local_back(ch):
         src, dst = back_refs(0, ch, 0)
@@ -298,81 +312,83 @@
         full_sum(j, ch, 0).wait_recv()
         full_sum(j, ch, 1).wait_recv()
         add(j, rds(core, y), BLOCK, ch, [BLOCK, 2 * BLOCK])
-        for dz in range(1, 4):
-            back(j, ch, dz).start()
-
-        @pl.when(j > 0)
-        def _():
-            back(j, ch, 0).start()
+        for k in range(1, 4):
+            back(j, ch, k).start()
+
+        if isinstance(j, int):
+            (back(j, ch, 0) if j else local_back(ch)).start()
+            return
+        back(j, ch, 0).start()
+
+    def early(j, carry):
+        forward_in(j, 0).wait_recv()
+        forward_in(j, 1).wait_recv()
+        share(j, 2, core).start()
+        for k in range(4):
+            share(j, k, other).wait_recv()
 
         @pl.when(j == 0)
         def _():
-            local_back(ch).start()
-
-    def credit(j):
-        @pl.when(j < CHUNKS - 2)
-        def _():
-            pl.semaphore_signal(cr_right, inc=1, device_id=left, device_id_type=MESH)
-            pl.semaphore_signal(cr_left, inc=1, device_id=right, device_id_type=MESH)
-
-    wait_weights(0)
-
-    def early(j, carry):
-        for half in (other, core):
-            gate_part, up_part = terms(j, half, 0)
-            gate_t[j, half_rows(half), :] = gate_part
-            up_t[j, half_rows(half), :] = up_part
+            wait_weights(0)
+
+        terms(j, other, 0)
+        terms(j, core, 0)
+        for direction in range(2):
+            own(j, direction).wait_send()
+            forward(j, direction).wait_send()
+        for k in range(4):
+            share(j, k, core).wait_send()
         return carry
 
     lax.fori_loop(0, CHUNKS, early, 0)
     wait_weights(1)
 
-    def step(j, carry):
-        last = terms(j, other, 1)
-        pl.semaphore_wait(cr_sib, 1)
-        for ch in range(2):
-            products(j, other, last, ch, False)
-            sib(j, ch).start()
-
-        @pl.when(j >= 1)
-        def _():
-            stage_half(j - 1, 1)
-
-        last = terms(j, core, 1)
-
-        @pl.when(j >= 1)
-        def _():
-            stage_full(j - 1, 0)
-
-        @pl.when(j >= 2)
-        def _():
+    def give(j, ch):
+        products(j, other, ch, False)
+        if ch == 0:
+            pl.semaphore_wait(cr_sib, 1)
+        sib(j, ch).start()
+
+    def take(j, ch):
+        sib(j, ch).wait_recv()
+        products(j, core, ch, True)
+        if ch == 0:
             pl.semaphore_wait(cr_right, 1)
             pl.semaphore_wait(cr_left, 1)
-
-        for ch in range(2):
-            sib(j, ch).wait_recv()
-            products(j, core, last, ch, True)
-            half_sum(j, ch, 0).start()
-            half_sum(j, ch, 1).start()
-
-        @pl.when(j < CHUNKS - 2)
-        def _():
-            pl.semaphore_signal(cr_sib, inc=1, device_id=sibling, device_id_type=MESH)
-
-        @pl.when(j >= 1)
-        def _():
-            stage_full(j - 1, 1)
-            credit(j - 1)
-
-        stage_half(j, 0)
+        half_sum(j, ch, 0).start()
+        half_sum(j, ch, 1).start()
+
+    def step(i, carry):
+        j = CHUNKS - 1 - i
+
+        def earlier(stage, ch):
+            @pl.when(i >= 1)
+            def _():
+                stage(j + 1, ch)
+
+        terms(j, other, 1)
+        pl.semaphore_signal(cr_sib, inc=1, device_id=sibling, device_id_type=MESH)
+        terms(j, core, 1)
+        pl.semaphore_signal(cr_right, inc=1, device_id=left, device_id_type=MESH)
+        pl.semaphore_signal(cr_left, inc=1, device_id=right, device_id_type=MESH)
+        give(j, 0)
+        earlier(stage_half, WIDTHS - 1)
+        for ch in range(1, WIDTHS):
+            give(j, ch)
+            take(j, ch - 1)
+            earlier(stage_full, ch - 1)
+        take(j, WIDTHS - 1)
+        earlier(stage_full, WIDTHS - 1)
+        for ch in range(WIDTHS - 1):
+            stage_half(j, ch)
         return carry
 
     lax.fori_loop(0, CHUNKS, step, 0)
-    stage_half(CHUNKS - 1, 1)
-    stage_full(CHUNKS - 1, 0)
-    stage_full(CHUNKS - 1, 1)
-
-    for ch in range(2):
+    stage_half(0, WIDTHS - 1)
+    for ch in range(WIDTHS):
+        stage_full(0, ch)
+
+    for ch in range(WIDTHS):
         local_back(ch).wait()
         for k in range(1, 16):
             back(k // 4, ch, k % 4).wait_recv()
@@ -384,12 +400,13 @@
 
         lax.fori_loop(0, WIDE // COLS, pick, 0)
 
-    for ch in range(2):
-        for k in range(1, 16):
+    for k in range(1, 16):
+        a2a(k // 4, k % 4).wait_send()
+        for ch in range(WIDTHS):
             back(k // 4, ch, k % 4).wait_send()
 
     def finish(j, carry):
-        for ch in range(2):
+        for ch in range(WIDTHS):
             sib(j, ch).wait_send()
             for direction in range(2):
                 half_sum(j, ch, direction).wait_send()
@@ -408,28 +425,28 @@
     return pl.pallas_call(
         kernel,
         out_shape=jax.ShapeDtypeStruct((n_tok, D), BF16),
-        in_specs=[vmem] * 4 + [hbm] * 3,
+        in_specs=[hbm] * 2 + [vmem] * 2 + [hbm] * 3,
         out_specs=vmem,
         scratch_shapes=[
             pltpu.VMEM((CHUNKS, 2, ROWS, D), BF16),
-            pltpu.VMEM((2, D, PART), BF16),
-            pltpu.VMEM((2, D, PART), BF16),
-            pltpu.VMEM((2, PART, D), BF16),
+            pltpu.VMEM((D, 2 * UNITS), BF16),
+            pltpu.VMEM((UNITS, D), BF16),
             pltpu.VMEM((2, HALF, D), BF16),
-            pltpu.VMEM((2, 3 * BLOCK, D), BF16),
             pltpu.VMEM((EXPERTS * SLOTS, D), BF16),
-            pltpu.VMEM((CHUNKS, ROWS, PART), BF16),
-            pltpu.VMEM((CHUNKS, ROWS, PART), BF16),
+            pltpu.VMEM((CHUNKS, ROWS, 2 * UNITS), BF16),
             pltpu.VMEM((n_tok, EXPERTS * SLOTS), BF16),
+            pltpu.VMEM((n_tok, D), BF16),
+            pltpu.VMEM((n_tok, D), BF16),
+            dma((2,)),
             dma((16,)), dma((16,)),
             dma((CHUNKS, 2)), dma((CHUNKS, 2)),
             dma((CHUNKS, 2)), dma((CHUNKS, 2)),
             dma((CHUNKS, 4)), dma((CHUNKS, 4)),
             dma((2, 3)), dma((2, 3)),
-            dma((CHUNKS, 2)), dma((CHUNKS, 2)),
-            dma((CHUNKS, 4)), dma((CHUNKS, 4)),
-            dma((CHUNKS, 4)), dma((CHUNKS, 4)),
-            dma((16, 2)), dma((16, 2)),
+            dma((CHUNKS, WIDTHS)), dma((CHUNKS, WIDTHS)),
+            dma((CHUNKS, 2 * WIDTHS)), dma((CHUNKS, 2 * WIDTHS)),
+            dma((CHUNKS, 2 * WIDTHS)), dma((CHUNKS, 2 * WIDTHS)),
+            dma((16, WIDTHS)), dma((16, WIDTHS)),
             regular, regular, regular,
         ],
         compiler_params=pltpu.CompilerParams(

time: 286 us -> 282 us (0.986); the launches traced: 282 us -> 282 us
  no operation moved by 1% of the time
where the time goes in v3:
time: 282 us
  Pallas kernels  280 us (99%)
    pallas_call x1, Pallas kernels, shards(): pl.pallas_call(kernel, out_shape=jax.ShapeDtypeStruct((n_tok, D), BF16),...  280 us

profile of v3, /device:TPU:96, one launch (start us, length us, event | category | flops | bytes accessed | tf_op | source)
XLA Modules:
  0.0 281.8 jit_solution(220283359323888378)
XLA Ops:
  0.0 279.5 %shard_map.73 = bf16[128,4096]{1,0:T(8,128)(2,1)} custom-call(bf16[128,4096]{1,0:T(8,128)(2,1)} %tok_h.1, bf16[128,4096]{1,0:T(8,128)(2,1)} %grad_h.1, f32[1,128]{1,0:T(1,128)} %bitcast.8, s32[1,128]{1,0:T(1,128)} %bitcast.9, bf16[4096,512]{1,0:T(8,128)(2,1)} %bitcast.5, bf16[4096,512]{1,0:T(8,128)(2,1)} %bitcast.6, bf16[512,4096]{1,0:T(8,128)(2,1)} %bitcast.7), custom_call_target="tpu_custom_call" | custom-call | flops 42949672960 | bytes 67108864 | tf_op jit(solution)/shard_map/pallas_call | solution.py:425
  279.5 2.3 copy.9

commit v4 on v3

--- a/solution.py
+++ b/solution.py
@@ -248,7 +248,7 @@
             rows[j, 0, rs, cs] = part.astype(BF16)
             return carry
 
-        lax.fori_loop(0, WIDE // COLS, columns, 0)
+        lax.fori_loop(0, WIDE // COLS, columns, 0, unroll=True)
 
     def landing(first, n):
         return pl.ds(pl.multiple_of(core * HALF + first, BLOCK // 2), n)
@@ -262,7 +262,7 @@
             rows[j, 0, at, cs] = total.astype(BF16)
             return carry
 
-        lax.fori_loop(0, WIDE // COLS, body, 0)
+        lax.fori_loop(0, WIDE // COLS, body, 0, unroll=True)
 
     def wide(ch):
         return pl.ds(ch * WIDE, WIDE)

time: 282 us -> 281 us (level)
  no operation moved by 1% of the time
where the time goes in v4:
time: 281 us
  Pallas kernels  278 us (99%)
    pallas_call x1, Pallas kernels, shards(): pl.pallas_call(kernel, out_shape=jax.ShapeDtypeStruct((n_tok, D), BF16),...  278 us

profile of v4, /device:TPU:96, one launch (start us, length us, event | category | flops | bytes accessed | tf_op | source)
XLA Modules:
  0.0 280.8 jit_solution(15153720173130161815)
XLA Ops:
  0.0 278.5 %shard_map.73 = bf16[128,4096]{1,0:T(8,128)(2,1)} custom-call(bf16[128,4096]{1,0:T(8,128)(2,1)} %tok_h.1, bf16[128,4096]{1,0:T(8,128)(2,1)} %grad_h.1, f32[1,128]{1,0:T(1,128)} %bitcast.8, s32[1,128]{1,0:T(1,128)} %bitcast.9, bf16[4096,512]{1,0:T(8,128)(2,1)} %bitcast.5, bf16[4096,512]{1,0:T(8,128)(2,1)} %bitcast.6, bf16[512,4096]{1,0:T(8,128)(2,1)} %bitcast.7), custom_call_target="tpu_custom_call" | custom-call | flops 42949672960 | bytes 67108864 | tf_op jit(solution)/shard_map/pallas_call | solution.py:425
  278.5 2.3 copy.9

commit v5 on v4

--- a/solution.py
+++ b/solution.py
@@ -52,7 +52,7 @@
 def kernel(
     tok_h, grad_h, prob, index, w_gate, w_up, w_down,
     out,
-    rows, gu_v, down_v, send, ret, terms_v, onehot_t, tok, grad, in_s,
+    rows, gu_v, down_v, send, ret, terms_v, onehot_t, tok, grad, in_s, out_s,
     a2a_s, a2a_r, ag_s, ag_r, fw_s, fw_r, sh_s, sh_r, w_s, w_r,
     sib_s, sib_r, half_s, half_r, full_s, full_r, ret_s, ret_r,
     cr_sib, cr_left, cr_right,
@@ -379,14 +379,22 @@
             earlier(stage_full, ch - 1)
         take(j, WIDTHS - 1)
         earlier(stage_full, WIDTHS - 1)
-        for ch in range(WIDTHS - 1):
-            stage_half(j, ch)
+        @pl.when(j > 0)
+        def _():
+            for ch in range(WIDTHS - 1):
+                stage_half(j, ch)
+
         return carry
 
     lax.fori_loop(0, CHUNKS, step, 0)
-    stage_half(0, WIDTHS - 1)
-    for ch in range(WIDTHS):
-        stage_full(0, ch)
+    for ch in range(WIDTHS + 2):
+        if ch < WIDTHS:
+            stage_half(0, ch)
+        if ch >= 2:
+            stage_full(0, ch - 2)
+
+    def result(ch):
+        return pltpu.make_async_copy(tok.at[:, wide(ch)], out.at[:, wide(ch)], out_s.at[ch])
 
     for ch in range(WIDTHS):
         local_back(ch).wait()
@@ -395,10 +403,11 @@
 
         def pick(n, carry):
             cs = pl.ds(pl.multiple_of(ch * WIDE + n * COLS, COLS), COLS)
-            out[:, cs] = jnp.dot(onehot_t[...], ret[:, cs], preferred_element_type=F32).astype(BF16)
+            tok[:, cs] = jnp.dot(onehot_t[...], ret[:, cs], preferred_element_type=F32).astype(BF16)
             return carry
 
-        lax.fori_loop(0, WIDE // COLS, pick, 0)
+        lax.fori_loop(0, WIDE // COLS, pick, 0, unroll=True)
+        result(ch).start()
 
     for k in range(1, 16):
         a2a(k // 4, k % 4).wait_send()
@@ -414,6 +423,8 @@
         return carry
 
     lax.fori_loop(0, CHUNKS, finish, 0)
+    for ch in range(WIDTHS):
+        result(ch).wait()
 
 
 def shards(tokens, grad_out, route_prob, expert_index, w_gate, w_up, w_down):
@@ -426,7 +437,7 @@
         kernel,
         out_shape=jax.ShapeDtypeStruct((n_tok, D), BF16),
         in_specs=[hbm] * 2 + [vmem] * 2 + [hbm] * 3,
-        out_specs=vmem,
+        out_specs=hbm,
         scratch_shapes=[
             pltpu.VMEM((CHUNKS, 2, ROWS, D), BF16),
             pltpu.VMEM((D, 2 * UNITS), BF16),
@@ -437,7 +448,7 @@
             pltpu.VMEM((n_tok, EXPERTS * SLOTS), BF16),
             pltpu.VMEM((n_tok, D), BF16),
             pltpu.VMEM((n_tok, D), BF16),
-            dma((2,)),
+            dma((2,)), dma((WIDTHS,)),
             dma((16,)), dma((16,)),
             dma((CHUNKS, 2)), dma((CHUNKS, 2)),
             dma((CHUNKS, 2)), dma((CHUNKS, 2)),

time: 281 us -> 280 us (level)
  no operation moved by 1% of the time
where the time goes in v5:
time: 280 us
  Pallas kernels  278 us (99%)
    pallas_call x1, Pallas kernels, shards(): pl.pallas_call(kernel, out_shape=jax.ShapeDtypeStruct((n_tok, D), BF16),...  278 us

profile of v5, /device:TPU:96, one launch (start us, length us, event | category | flops | bytes accessed | tf_op | source)
XLA Modules:
  0.0 280.1 jit_solution(11377870652035908916)
XLA Ops:
  0.0 277.8 %shard_map.73 = bf16[128,4096]{1,0:T(8,128)(2,1)} custom-call(bf16[128,4096]{1,0:T(8,128)(2,1)} %tok_h.1, bf16[128,4096]{1,0:T(8,128)(2,1)} %grad_h.1, f32[1,128]{1,0:T(1,128)} %bitcast.8, s32[1,128]{1,0:T(1,128)} %bitcast.9, bf16[4096,512]{1,0:T(8,128)(2,1)} %bitcast.5, bf16[4096,512]{1,0:T(8,128)(2,1)} %bitcast.6, bf16[512,4096]{1,0:T(8,128)(2,1)} %bitcast.7), custom_call_target="tpu_custom_call" | custom-call | flops 42949672960 | bytes 67108864 | tf_op jit(solution)/shard_map/pallas_call | solution.py:436
  277.9 2.3 copy.9
